TPU v7x, 32 devices: a whole 2x2x4 slice. The times are simulated.
32 devices in a mesh: groups: 1, ep: 32 (over z, y, x, core).
Axes of the slice: x: 2, y: 2, z: 4, core: 2. Of those that a mesh axis runs over, the one named last changes fastest.
Arguments:
- hidden_in: bfloat16 [640, 2048], P(('groups', 'ep')), may hold values from -6 to 6
- queries: bfloat16 [640, 2048], P(('groups', 'ep')), may hold values from -6 to 6
- key_rows: bfloat16 [640, 2048], P(('groups', 'ep')), may hold values from -6 to 6
- value_rows: bfloat16 [640, 2048], P(('groups', 'ep')), may hold values from -6 to 6
- output_gate: bfloat16 [640, 2048], P(('groups', 'ep')), may hold values from -6 to 6
- decay_rate: float32 [640, 16], P(('groups', 'ep')), may hold values from 0.2 to 1
- write_rate: float32 [640, 16], P(('groups', 'ep')), may hold values from 0.1 to 1
- state_cache: bfloat16 [128, 16, 128, 128], P(('groups', 'ep')), may hold values from -6 to 6
- head_gain: float32 [128], replicated, may hold values from 0.25 to 1.75
- post_gain: float32 [2048], replicated, may hold values from 0.25 to 1.75
- routes: int32 [640, 10], P(('groups', 'ep')), may hold values from 0 to 31, all different within a row; in each aligned block of 20 rows (0 to 19, 20 to 39, ...) at most 7 rows name the same one
- route_weight: float32 [640, 10], P(('groups', 'ep')), may hold values from 0.05 to 0.3
- w_gate_up: bfloat16 [32, 2048, 1024], P('ep'), may hold values from -0.125 to 0.125
- w_down: bfloat16 [32, 512, 2048], P('ep'), may hold values from -0.25 to 0.25
Outputs:
- layer_out: bfloat16 [640, 2048], P(('groups', 'ep'))
Inputs may be any that keep to these rules, and one draw needn't show every extreme that they name: `routes`: in each aligned block of 20 rows (the rows of one device) a row names 10 different experts and no expert is named more than 7 times; in every draw some expert is named exactly 7 times in some block.
All inputs are finite; a program needn't handle non-finite values.
Results may differ from a plain program's by a relative error of at most 0.0037.
Values may be sent and summed in bfloat16 or wider, within the bound.
A program may use at most 64 MiB of HBM per device.

v0:
```python
import jax
import jax.numpy as jnp
from jax import lax
from jax.sharding import PartitionSpec as P


def normalize(vectors):
    return vectors / jnp.sqrt(jnp.sum(vectors * vectors, -1, keepdims=True) + 1e-06)


def attend(
    hidden_in,
    queries,
    key_rows,
    value_rows,
    output_gate,
    decay_rate,
    write_rate,
    state_cache,
    head_gain,
    post_gain,
):
    count, heads = decay_rate.shape
    seq_count = state_cache.shape[0]
    steps = count // seq_count
    head_dim = head_gain.shape[0]
    q_unit = normalize(queries.astype(jnp.float32).reshape(seq_count, steps, heads, head_dim))
    k_unit = normalize(key_rows.astype(jnp.float32).reshape(seq_count, steps, heads, head_dim))
    values = value_rows.astype(jnp.float32).reshape(seq_count, steps, heads, head_dim)
    gating = output_gate.astype(jnp.float32).reshape(count, heads, head_dim)
    decays = decay_rate.reshape(seq_count, steps, heads)
    writes = write_rate.reshape(seq_count, steps, heads)
    state = state_cache.astype(jnp.float32)
    outputs = []
    for step in range(steps):
        q_now = q_unit[:, step]
        k_now = k_unit[:, step]
        v_now = values[:, step]
        alpha = decays[:, step][..., None]
        beta = writes[:, step][..., None]
        stacked = jnp.stack([q_now, k_now], 1)
        reads = jnp.einsum(
            "rshk,rhkv->rshv",
            stacked,
            state,
            precision=lax.Precision.HIGHEST,
            preferred_element_type=jnp.float32,
        )
        q_read = reads[:, 0]
        k_read = reads[:, 1]
        intersection = jnp.sum(q_now * k_now, -1, keepdims=True)
        outputs.append(alpha * q_read + beta * intersection * (v_now - alpha * k_read))
        state = (
            alpha[..., None] * (state - beta[..., None] * k_now[..., None] * k_read[:, :, None, :])
            + beta[..., None] * k_now[..., None] * v_now[:, :, None, :]
        )
    attn = jnp.stack(outputs, 1).reshape(count, heads, head_dim)
    scale = lax.rsqrt(jnp.mean(attn * attn, -1, keepdims=True) + 1e-06)
    gated = attn * scale * head_gain * jax.nn.silu(gating)
    mixed = hidden_in.astype(jnp.float32) + gated.reshape(count, heads * head_dim)
    factor = lax.rsqrt(jnp.mean(mixed * mixed, -1, keepdims=True) + 1e-06)
    normed = (mixed * factor * post_gain).astype(jnp.bfloat16)
    return (mixed, normed)


def expert_block(normed, routes, route_weight, w_gate_up, w_down, capacity):
    row_count, top_count = routes.shape
    width = normed.shape[1]
    expert_count = lax.axis_size("ep")
    flat_routes = routes.reshape(-1)
    position = jnp.arange(row_count * top_count, dtype=jnp.int32)
    earlier = (flat_routes[:, None] == flat_routes[None, :]) & (
        position[:, None] > position[None, :]
    )
    rank = jnp.sum(earlier.astype(jnp.int32), -1)
    slot = flat_routes * capacity + rank
    slot_ids = jnp.arange(expert_count * capacity, dtype=jnp.int32)
    slot_route = (slot[None, :] == slot_ids[:, None]).astype(jnp.bfloat16)
    route_row = (
        (position // top_count)[:, None] == jnp.arange(row_count, dtype=jnp.int32)[None, :]
    ).astype(jnp.bfloat16)
    selector = jnp.dot(slot_route, route_row, preferred_element_type=jnp.float32).astype(
        jnp.bfloat16
    )
    outgoing = jnp.dot(selector, normed, preferred_element_type=jnp.float32).astype(jnp.bfloat16)
    outgoing = outgoing.reshape(expert_count, capacity, width)
    arrived = lax.all_to_all(outgoing, "ep", split_axis=0, concat_axis=0, tiled=True)
    hidden_width = w_down.shape[1]
    product = jnp.dot(arrived.reshape(-1, width), w_gate_up[0], preferred_element_type=jnp.float32)
    hidden_units = (jax.nn.silu(product[:, :hidden_width]) * product[:, hidden_width:]).astype(
        jnp.bfloat16
    )
    results = jnp.dot(hidden_units, w_down[0], preferred_element_type=jnp.float32).astype(
        jnp.bfloat16
    )
    returned = lax.all_to_all(
        results.reshape(expert_count, capacity, width),
        "ep",
        split_axis=0,
        concat_axis=0,
        tiled=True,
    )
    picked = returned.reshape(-1, width)[slot].reshape(row_count, top_count, width)
    return jnp.sum(route_weight[..., None] * picked.astype(jnp.float32), 1)


def per_device(
    hidden_in,
    queries,
    key_rows,
    value_rows,
    output_gate,
    decay_rate,
    write_rate,
    state_cache,
    head_gain,
    post_gain,
    routes,
    route_weight,
    w_gate_up,
    w_down,
):
    row_total = hidden_in.shape[0]
    top_count = routes.shape[1]
    expert_count = lax.axis_size("ep")
    capacity = max(2, (row_total * top_count + expert_count - 1) // expert_count)
    mixed, normed = attend(
        hidden_in,
        queries,
        key_rows,
        value_rows,
        output_gate,
        decay_rate,
        write_rate,
        state_cache,
        head_gain,
        post_gain,
    )
    moe_sum = expert_block(normed, routes, route_weight, w_gate_up, w_down, capacity)
    return (mixed + moe_sum).astype(jnp.bfloat16)


def solution(mesh):
    in_specs = (
        P(("groups", "ep"), None),
        P(("groups", "ep"), None),
        P(("groups", "ep"), None),
        P(("groups", "ep"), None),
        P(("groups", "ep"), None),
        P(("groups", "ep"), None),
        P(("groups", "ep"), None),
        P(("groups", "ep"), None, None, None),
        P(),
        P(),
        P(("groups", "ep"), None),
        P(("groups", "ep"), None),
        P("ep", None, None),
        P("ep", None, None),
    )
    out_specs = P(("groups", "ep"), None)
    return jax.shard_map(
        per_device, mesh=mesh, in_specs=in_specs, out_specs=out_specs, check_vma=False
    )
```

profile of v0, /device:TPU:0, one launch (start us, length us, event | category | flops | bytes accessed | tf_op | source)
XLA Modules:
  0.0 124.2 jit_solution(16779897487012114672)
XLA Ops:
  0.0 0.9 copy.104
  1.0 0.9 reshape.258
  2.2 0.9 reshape.260
  3.5 0.2 bitcast_multiply_fusion.2
  4.0 3.3 %convolution_bitcast_fusion = f32[4,2,16,128]{3,1,2,0:T(2,128)S(1)} fusion(bf16[4,16,128,128]{3,2,1,0:T(8,128)(2,1)} %param.21, f32[4,1,16,128]{3,1,2,0:T(1,128)S(1)} %bitcast.120, f32[4,1,16,128]{3,1,2,0:T(1,128)S(1)} %bitcast.119), kind=kOutput, calls=%fused_computation.39 | convolution fusion | flops 25182208 | bytes 2228224 | tf_op jit(solution)/shard_map/rshk,rhkv->rshv/dot_general | solution.py:42
  7.4 0.2 fusion.73
  7.6 6.2 %fusion.30 = f32[4,2,16,128]{3,1,2,0:T(2,128)S(1)} fusion(bf16[4,16,128,128]{3,2,1,0:T(8,128)(2,1)} %param.21, f32[4,16,128]{2,1,0:T(8,128)S(1)} %get-tuple-element.23, f32[4,16,128]{2,1,0:T(8,128)S(1)} %bitcast.126, f32[4,16,128]{2,1,0:T(8,128)S(1)} %get-tuple-element.33, f32[4,16]{1,0:T(4,128)S(1)} %bitcast.156, f32[4,2,16,128]{3,2,0,1:T(8,128)S(1)} %get-tuple-element.57), kind=kOutput, calls=%fused_computation.37 | convolution fusion | flops 31457280 | bytes 2326784 | tf_op jit(solution)/shard_map/rshk,rhkv->rshv/dot_general | solution.py:42
  13.8 0.2 fusion.72
  14.0 6.6 %fusion.28 = f32[4,2,16,128]{3,1,2,0:T(2,128)S(1)} fusion(bf16[4,16,128,128]{3,2,1,0:T(8,128)(2,1)S(1)} %copy-done.1, f32[4,16,128]{2,1,0:T(8,128)S(1)} %get-tuple-element.24, f32[4,16,128]{2,1,0:T(8,128)S(1)} %bitcast.130, f32[4,16,128]{2,1,0:T(8,128)S(1)} %get-tuple-element.32, f32[4,16]{1,0:T(4,128)S(1)} %bitcast.152, ...), kind=kOutput, calls=%fused_computation.35 | convolution fusion | flops 36700160 | bytes 2425344 | tf_op jit(solution)/shard_map/rshk,rhkv->rshv/dot_general | solution.py:42
  20.6 0.2 fusion.71
  20.9 7.8 %fusion.29 = f32[4,2,16,128]{3,1,2,0:T(2,128)S(1)} fusion(f32[4,16,128]{2,1,0:T(8,128)S(1)} %get-tuple-element.25, f32[4,16,128]{2,1,0:T(8,128)S(1)} %bitcast.133, f32[4,16,128]{2,1,0:T(8,128)S(1)} %get-tuple-element.34, f32[4,16]{1,0:T(4,128)S(1)} %bitcast.149, f32[4,16,128]{2,1,0:T(8,128)S(1)} %get-tuple-element.24, f32[4,16,128]{2,1,0:T(8,128)S(1)} %bitcast.131, ...), kind=kOutput, calls=%fused_computation.36 | convolution fusion | flops 41943040 | bytes 2523904 | tf_op jit(solution)/shard_map/rshk,rhkv->rshv/dot_general | solution.py:42
  28.7 0.2 fusion.70
  29.0 10.8 %fusion.31 = f32[4,2,16,128]{3,1,2,0:T(2,128)S(1)} fusion(f32[4,16,128]{2,1,0:T(8,128)S(1)} %get-tuple-element.26, f32[4,16,128]{2,1,0:T(8,128)S(1)} %bitcast.135, f32[4,16,128]{2,1,0:T(8,128)S(1)} %get-tuple-element.31, f32[4,16]{1,0:T(4,128)S(1)} %bitcast.147, f32[4,16,128]{2,1,0:T(8,128)S(1)} %get-tuple-element.25, f32[4,16,128]{2,1,0:T(8,128)S(1)} %bitcast.134, ...), kind=kOutput, calls=%fused_computation.38 | convolution fusion | flops 47185920 | bytes 2622464 | tf_op jit(solution)/shard_map/rshk,rhkv->rshv/dot_general | solution.py:42
  39.8 0.2 fusion.57
  40.1 0.2 stack.28
  40.3 0.1 multiply_reduce_fusion.1
  41.0 0.2 multiply_reduce_fusion.2
  41.4 0.2 convert_reduce_fusion
  41.6 1.7 %convolution_convert_fusion.1 = bf16[224,2048]{1,0:T(8,128)(2,1)} fusion(s32[200]{0:T(256)S(1)} %get-tuple-element.62, f32[20,2048]{1,0:T(8,128)S(1)} %get-tuple-element.10, f32[2048]{0:T(1024)S(1)} %copy-done.6, f32[20]{0:T(128)S(1)} %add_rsqrt_fusion.1, s32[200]{0:T(256)S(1)} %get-tuple-element.61), kind=kOutput, calls=%fused_computation.16 | convolution fusion | flops 20776992 | bytes 1091216 | tf_op jit(solution)/shard_map/dot_general | solution.py:85
  43.2 1.5 %reshape.254 = bf16[32,7,2048]{2,1,0:T(8,128)(2,1)S(1)} reshape(bf16[224,2048]{1,0:T(8,128)(2,1)} %convolution_convert_fusion.1) | data formatting | bytes 1835008 | tf_op jit(solution)/shard_map/reshape | solution.py:86
  44.7 33.5 %all_to_all.10 = bf16[32,7,2048]{2,1,0:T(8,128)(2,1)} all-to-all(bf16[32,7,2048]{2,1,0:T(8,128)(2,1)S(1)} %reshape.254), channel_id=1, replica_groups=mesh['groups'=1,'ep'=32] {'ep'}, dimensions={0} | all-to-all | bytes 1835008 | tf_op jit(solution)/shard_map/all_to_all | solution.py:87
  78.2 1.5 %reshape.255 = bf16[224,2048]{1,0:T(8,128)(2,1)S(1)} reshape(bf16[32,7,2048]{2,1,0:T(8,128)(2,1)} %all_to_all.10) | data formatting | bytes 1835008 | tf_op jit(solution)/shard_map/reshape | solution.py:89
  79.7 3.3 %fusion = f32[224,1024]{1,0:T(8,128)S(1)} fusion(bf16[224,2048]{1,0:T(8,128)(2,1)S(1)} %reshape.255, bf16[1,2048,1024]{2,1,0:T(8,128)(2,1)} %param.26), kind=kOutput, calls=%fused_computation.1 | convolution fusion | flops 939524096 | bytes 6029312 | tf_op jit(solution)/shard_map/dot_general | solution.py:89
  83.0 0.7 convolution_convert_fusion
  83.7 1.3 %reshape.256 = bf16[32,7,2048]{2,1,0:T(8,128)(2,1)} reshape(bf16[224,2048]{1,0:T(8,128)(2,1)S(1)} %convolution_convert_fusion) | data formatting | bytes 1835008 | tf_op jit(solution)/shard_map/reshape | solution.py:97
  85.0 3.8 %all-to-all-start.1 = ((bf16[32,7,2048]{2,1,0:T(8,128)(2,1)}), bf16[32,7,2048]{2,1,0:T(8,128)(2,1)}, u32[]{:S(2)}, u32[]{:S(2)}) async-start(bf16[32,7,2048]{2,1,0:T(8,128)(2,1)} %reshape.256), calls=%async_computation.1 | async-start | bytes 2097152 | tf_op jit(solution)/shard_map/all_to_all | solution.py:96
  89.1 25.9 %all-to-all-done.1 = bf16[32,7,2048]{2,1,0:T(8,128)(2,1)} async-done(((bf16[32,7,2048]{2,1,0:T(8,128)(2,1)}), bf16[32,7,2048]{2,1,0:T(8,128)(2,1)}, u32[]{:S(2)}, u32[]{:S(2)}) %all-to-all-start.1) | async-done | bytes 917536 | tf_op jit(solution)/shard_map/all_to_all | solution.py:96
  115.0 1.5 %reshape.257 = bf16[224,2048]{1,0:T(8,128)(2,1)S(1)} reshape(bf16[32,7,2048]{2,1,0:T(8,128)(2,1)} %all-to-all-done.1) | data formatting | bytes 1835008 | tf_op jit(solution)/shard_map/reshape | solution.py:103
  116.5 2.1 %gather_fusion = bf16[200,2048]{1,0:T(8,128)(2,1)} fusion(bf16[224,2048]{1,0:T(8,128)(2,1)S(1)} %reshape.257, s32[1024]{0:T(1024)S(1)} %pad_clamp_fusion), kind=kCustom, calls=%fused_computation | custom fusion | bytes 1639200 | tf_op jit(solution)/shard_map/gather | solution.py:103
  118.6 2.7 %reshape.264 = f32[20,10,2048]{2,1,0:T(8,128)} reshape(bf16[200,2048]{1,0:T(8,128)(2,1)} %gather_fusion) | data formatting | bytes 2457600 | tf_op jit(solution)/shard_map/convert_element_type | solution.py:104
  121.2 2.3 %multiply_reduce_fusion = f32[20,2048]{1,0:T(8,128)S(1)} fusion(f32[20,10,2048]{2,1,0:T(8,128)} %reshape.264, f32[20,10]{1,0:T(8,128)S(1)} %copy.116), kind=kLoop, calls=%fused_computation.14 | loop fusion | flops 778240 | bytes 1803040 | tf_op jit(solution)/shard_map/reduce_sum | solution.py:104
  123.5 0.7 add_convert_fusion
  (69 shorter events, 1.9 us)
Async XLA Ops:
  0.0 83.0 %copy-start = (bf16[1,512,2048]{2,1,0:T(8,128)(2,1)S(1)}, bf16[1,512,2048]{2,1,0:T(8,128)(2,1)}, u32[]{:S(2)}) copy-start(bf16[1,512,2048]{2,1,0:T(8,128)(2,1)} %param.27) | copy-start | bytes 6291460
  0.0 3.7 %copy-start.2 = (bf16[20,2048]{1,0:T(8,128)(2,1)S(1)}, bf16[20,2048]{1,0:T(8,128)(2,1)}, u32[]{:S(2)}) copy-start(bf16[20,2048]{1,0:T(8,128)(2,1)} %param.17) | copy-start | bytes 245764
  0.0 3.9 %copy-start.7 = (f32[20,16]{0,1:T(8,128)S(1)}, f32[20,16]{0,1:T(8,128)}, u32[]{:S(2)}) copy-start(f32[20,16]{0,1:T(8,128)} %param.19) | copy-start | bytes 3844
  7.3 6.6 %copy-start.1 = (bf16[4,16,128,128]{3,2,1,0:T(8,128)(2,1)S(1)}, bf16[4,16,128,128]{3,2,1,0:T(8,128)(2,1)}, u32[]{:S(2)}) copy-start(bf16[4,16,128,128]{3,2,1,0:T(8,128)(2,1)} %param.21) | copy-start | bytes 6291460
  28.9 12.0 %copy-start.9 = (f32[128]{0:T(128)S(1)}, f32[128]{0:T(128)}, u32[]{:S(2)}) copy-start(f32[128]{0:T(128)} %param.22) | copy-start | bytes 1540
  29.0 12.0 %copy-start.3 = (bf16[20,2048]{1,0:T(8,128)(2,1)S(1)}, bf16[20,2048]{1,0:T(8,128)(2,1)}, u32[]{:S(2)}) copy-start(bf16[20,2048]{1,0:T(8,128)(2,1)} %param.18) | copy-start | bytes 245764
  29.0 12.0 %copy-start.4 = (bf16[20,2048]{1,0:T(8,128)(2,1)S(1)}, bf16[20,2048]{1,0:T(8,128)(2,1)}, u32[]{:S(2)}) copy-start(bf16[20,2048]{1,0:T(8,128)(2,1)} %param.14) | copy-start | bytes 245764
  29.0 12.2 %copy-start.5 = (s32[20,10]{0,1:T(8,128)S(1)}, s32[20,10]{0,1:T(8,128)}, u32[]{:S(2)}) copy-start(s32[20,10]{0,1:T(8,128)} %param.24) | copy-start | bytes 2404
  29.0 12.6 %copy-start.6 = (f32[2048]{0:T(1024)S(1)}, f32[2048]{0:T(1024)}, u32[]{:S(2)}) copy-start(f32[2048]{0:T(1024)} %param.23) | copy-start | bytes 24580
  83.0 6.0 %copy-start.8 = (f32[20,10]{0,1:T(8,128)S(1)}, f32[20,10]{0,1:T(8,128)}, u32[]{:S(2)}) copy-start(f32[20,10]{0,1:T(8,128)} %param.25) | copy-start | bytes 2404
  85.0 30.0 %all-to-all-start.1 = ((bf16[32,7,2048]{2,1,0:T(8,128)(2,1)}), bf16[32,7,2048]{2,1,0:T(8,128)(2,1)}, u32[]{:S(2)}, u32[]{:S(2)}) async-start(bf16[32,7,2048]{2,1,0:T(8,128)(2,1)} %reshape.256), calls=%async_computation.1 | async-start | bytes 2097152 | tf_op jit(solution)/shard_map/all_to_all | solution.py:96
where the time goes:
time: 125 us; the launch traced here: 124 us
  matrix products  40.5 us (32%)
  blocking collectives  33.5 us (27%)
  waiting for transfers between devices  25.9 us (21%)
  local copies, waits for them, and re-layouts  12.9 us (10%)
  other arithmetic  7.22 us (6%)
  starting transfers between devices  3.75 us (3%)
    dot_general x5, matrix products, attend(): jnp.einsum('rshk,rhkv->rshv', stacked, state, precision=lax.Precision.HIG...  34.8 us
    all_to_all x1, blocking collectives, expert_block(): lax.all_to_all(outgoing, 'ep', split_axis=0, concat_axis=0, tiled=True)  33.5 us
    all_to_all x1, waiting for transfers between devices, expert_block(): lax.all_to_all(results.reshape(expert_count, capacity, width), 'ep', spli...  25.9 us
    all_to_all x1, starting transfers between devices, expert_block(): lax.all_to_all(results.reshape(expert_count, capacity, width), 'ep', spli...  3.75 us
    dot_general x1, matrix products, expert_block(): jnp.dot(arrived.reshape(-1, width), w_gate_up[0], preferred_element_type=...  3.3 us
    convert_element_type x1, local copies, waits for them, and re-layouts, expert_block(): return jnp.sum(route_weight[..., None] * picked.astype(jnp.float32), 1)  2.67 us
  transfers between devices with their start and end apart: 1, of which 1 were waited for; matrix products, arithmetic and copies ran while one was open for 0% of the time, Pallas kernels for 0%

commit v1 on v0

v1 whole, which is shorter than its diff:
```python
import functools

import jax
import jax.numpy as jnp
from jax import lax
from jax.experimental import pallas as pl
from jax.experimental.pallas import tpu as pltpu
from jax.sharding import PartitionSpec as P

F32 = jnp.float32
BF16 = jnp.bfloat16
LANE = 8
MESH = pl.DeviceIdType.MESH


def iota(shape, dim):
    return lax.broadcasted_iota(jnp.int32, shape, dim)


def exact_dot(a, b, dims=None):
    dims = dims or (((1,), (0,)), ((), ()))
    return lax.dot_general(a, b, dims, precision=lax.Precision.HIGHEST, preferred_element_type=F32)


def dot(a, b):
    return jnp.dot(a, b, preferred_element_type=F32)


def split(value):
    high = value.astype(BF16)
    return high, (value - high.astype(F32)).astype(BF16)


def kernel(
    n,
    steps,
    heads,
    head_dim,
    hidden_ref,
    q_ref,
    k_ref,
    v_ref,
    gate_ref,
    decay_ref,
    write_ref,
    state_ref,
    head_gain_ref,
    post_gain_ref,
    routes_ref,
    weight_ref,
    gate_up_hbm,
    down_hbm,
    out_ref,
    hid_s,
    q_s,
    k_s,
    v_s,
    gate_s,
    a_s,
    b_s,
    mixed_s,
    gate_up_s,
    down_s,
    out_buf,
    in_buf,
    back_buf,
    ret_buf,
    hidden_s,
    weight_sem,
    local_sem,
    send_sem,
    recv_sem,
):
    me = lax.axis_index("ep")
    rows, width = hidden_ref.shape
    top = routes_ref.shape[1]
    seqs = rows // steps
    packed = steps * LANE
    half = width // 2
    ff = down_s.shape[0]
    barrier = pltpu.get_barrier_semaphore()

    def greet(i, carry):
        pl.semaphore_signal(
            barrier, inc=1, device_id={"ep": lax.rem(me + i, n)}, device_id_type=MESH
        )
        return carry

    lax.fori_loop(1, n, greet, 0)
    gate_up_copy = pltpu.make_async_copy(gate_up_hbm.at[0], gate_up_s, weight_sem.at[0])
    down_copy = pltpu.make_async_copy(down_hbm.at[0], down_s, weight_sem.at[1])
    gate_up_copy.start()
    down_copy.start()

    new_row, old_row = iota((packed, rows), 0), iota((packed, rows), 1)
    place = (old_row // steps == new_row % LANE) & (old_row % steps == new_row // LANE)
    place_f = place.astype(F32)
    place_b = place_f.astype(BF16)
    hid_s[...] = dot(place_b, hidden_ref[...])
    q_s[...] = dot(place_b, q_ref[...])
    k_s[...] = dot(place_b, k_ref[...])
    v_s[...] = dot(place_b, v_ref[...])
    gate_s[...] = dot(place_b, gate_ref[...])
    spread = (iota((heads, width), 1) // head_dim == iota((heads, width), 0)).astype(F32)
    a_s[...] = exact_dot(exact_dot(place_f, decay_ref[...]), spread)
    b_s[...] = exact_dot(exact_dot(place_f, write_ref[...]), spread)
    gain = head_gain_ref[...]
    sequence = iota((2 * packed, head_dim), 0) % LANE

    def lanes_sum(value):
        return jnp.sum(value, -1, keepdims=True)

    def one_head(h):
        cols = pl.ds(pl.multiple_of(h * head_dim, head_dim), head_dim)
        k_all, q_all = k_s[:, cols], q_s[:, cols]
        both = jnp.concatenate([k_all, q_all], 0).astype(BF16)
        reads = jnp.zeros((2 * packed, head_dim), F32)
        for s in range(seqs):
            reads = jnp.where(sequence == s, dot(both, state_ref[s, h]), reads)
        carried = None
        writes, keys = [], []
        for t in range(steps):
            at = slice(t * LANE, (t + 1) * LANE)
            k, q = k_all[at], q_all[at]
            here = pl.ds(t * LANE, LANE)
            a, b, v = a_s[here, cols], b_s[here, cols], v_s[here, cols]
            k_scale = lax.rsqrt(lanes_sum(k * k) + 1e-06)
            q_scale = lax.rsqrt(lanes_sum(q * q) + 1e-06)
            k_read = reads[at] if t == 0 else carried * reads[at]
            for key, w in zip(keys, writes):
                k_read = k_read + lanes_sum(k * key) * w
            new = b * (v - a * (k_scale * k_read))
            carried = a if t == 0 else carried * a
            writes = [w * a for w in writes] + [new * k_scale]
            keys = keys + [k]
            attn = carried * reads[packed + t * LANE : packed + (t + 1) * LANE]
            for key, w in zip(keys, writes):
                attn = attn + lanes_sum(q * key) * w
            attn = attn * q_scale
            norm = lax.rsqrt(lanes_sum(attn * attn) * (1.0 / head_dim) + 1e-06)
            g = gate_s[here, cols]
            mixed_s[here, cols] = hid_s[here, cols] + attn * norm * gain * (g / (1.0 + jnp.exp(-g)))

    def head_group(i, carry):
        for j in range(2):
            one_head(2 * i + j)
        return carry

    lax.fori_loop(0, heads // 2, head_group, 0)
    mixed = mixed_s[...]
    factor = lax.rsqrt(jnp.sum(mixed * mixed, -1, keepdims=True) * (1.0 / width) + 1e-06)
    normed = (mixed * factor * post_gain_ref[...]).astype(BF16)

    expert = iota((rows, n), 1)
    named = jnp.zeros((rows, n), F32)
    weights = jnp.zeros((rows, n), F32)
    for j in range(top):
        hit = routes_ref[:, j : j + 1] == expert
        named = jnp.where(hit, 1.0, named)
        weights = jnp.where(hit, weight_ref[:, j : j + 1], weights)
    earlier = (iota((rows, rows), 0) >= iota((rows, rows), 1)).astype(BF16)
    order = named * dot(earlier, named.astype(BF16))
    order = dot(place_b, order.astype(BF16)).astype(BF16)
    weights = exact_dot(place_f, weights)

    slots = n * 16
    slot_row = iota((slots, n), 0)
    owner = (slot_row // 16 == iota((slots, n), 1)).astype(BF16)
    found = lax.dot_general(owner, order, (((1,), (1,)), ((), ())), preferred_element_type=F32)
    slot_at = iota((slots, packed), 0)
    chosen = found == (slot_at % 8 + 1).astype(F32)
    on_left = slot_at % 16 < 8
    pick_left = jnp.where(chosen & on_left, 1.0, 0.0).astype(BF16)
    pick_right = jnp.where(chosen & ~on_left, 1.0, 0.0).astype(BF16)
    step = 256
    for c in range(half // step):
        left = normed[:, c * step : (c + 1) * step]
        right = normed[:, half + c * step : half + (c + 1) * step]
        out_buf[:, c * step : (c + 1) * step] = (dot(pick_left, left) + dot(pick_right, right)).astype(BF16)

    def block(i):
        return pl.ds(pl.multiple_of(i * 16, 16), 16)

    def exchange(source, target, number):
        def send(i, carry):
            other = lax.rem(me + i, n)
            pltpu.make_async_remote_copy(
                src_ref=source.at[block(other)],
                dst_ref=target.at[block(me)],
                send_sem=send_sem.at[number],
                recv_sem=recv_sem.at[number],
                device_id={"ep": other},
                device_id_type=MESH,
            ).start()
            return carry

        lax.fori_loop(1, n, send, 0)
        own = pltpu.make_async_copy(source.at[block(me)], target.at[block(me)], local_sem.at[number])
        own.start()
        own.wait()
        rest = pl.ds(0, (n - 1) * 16)
        return pltpu.make_async_remote_copy(
            src_ref=source.at[rest],
            dst_ref=target.at[rest],
            send_sem=send_sem.at[number],
            recv_sem=recv_sem.at[number],
            device_id={"ep": lax.rem(me + 1, n)},
            device_id_type=MESH,
        )

    pl.semaphore_wait(barrier, n - 1)
    first = exchange(out_buf, in_buf, 0)
    owner_t = (iota((n, slots), 1) // 16 == iota((n, slots), 0)).astype(BF16)
    lane_slot = iota((packed, slots), 1)
    taken = dot(order, owner_t) == (lane_slot % 8 + 1).astype(F32)
    high, low = split(weights)
    lane_left = lane_slot % 16 < 8
    mixing = []
    for part in (high, low):
        value = dot(part, owner_t)
        mixing.append(jnp.where(taken & lane_left, value, 0.0).astype(BF16))
        mixing.append(jnp.where(taken & ~lane_left, value, 0.0).astype(BF16))
    mix = jnp.concatenate(mixing, 0)
    gate_up_copy.wait()
    down_copy.wait()
    first.wait_recv()

    arrived = in_buf[...].astype(F32).reshape(n, 16, half)
    left_in = arrived[:, :8].reshape(n * 8, half).astype(BF16)
    right_in = arrived[:, 8:].reshape(n * 8, half).astype(BF16)
    for c in range(ff // step):
        at = slice(c * step, (c + 1) * step)
        up_at = slice(ff + c * step, ff + (c + 1) * step)
        gate = dot(left_in, gate_up_s[:half, at]) + dot(right_in, gate_up_s[half:, at])
        up = dot(left_in, gate_up_s[:half, up_at]) + dot(right_in, gate_up_s[half:, up_at])
        hidden_s[:, at] = (gate / (1.0 + jnp.exp(-gate)) * up).astype(BF16)
    units = hidden_s[...]
    for c in range(half // step):
        at = slice(c * step, (c + 1) * step)
        right_at = slice(half + c * step, half + (c + 1) * step)
        left = dot(units, down_s[:, at]).reshape(n, 8, step)
        right = dot(units, down_s[:, right_at]).reshape(n, 8, step)
        back_buf[:, at] = jnp.concatenate([left, right], 1).reshape(slots, step).astype(BF16)
    second = exchange(back_buf, ret_buf, 1)
    first.wait_send()
    second.wait_recv()
    for c in range(half // step):
        at = slice(c * step, (c + 1) * step)
        right_at = slice(half + c * step, half + (c + 1) * step)
        sums = dot(mix, ret_buf[:, at])
        left = sums[:packed] + sums[2 * packed : 3 * packed]
        right = sums[packed : 2 * packed] + sums[3 * packed :]
        for cols, value in ((at, left), (right_at, right)):
            total = (mixed_s[:, cols] + value).astype(BF16)
            out_ref[:, cols] = lax.dot_general(
                place_b, total, (((0,), (0,)), ((), ())), preferred_element_type=F32
            ).astype(BF16)
    second.wait_send()


def per_device(
    hidden_in,
    queries,
    key_rows,
    value_rows,
    output_gate,
    decay_rate,
    write_rate,
    state_cache,
    head_gain,
    post_gain,
    routes,
    route_weight,
    w_gate_up,
    w_down,
):
    rows, width = hidden_in.shape
    n = lax.axis_size("ep")
    seqs, heads, head_dim, _ = state_cache.shape
    steps = rows // seqs
    packed = steps * LANE
    ff = w_down.shape[1]
    capacity = max(2, (rows * routes.shape[1] + n - 1) // n)
    assert capacity <= 8 and seqs <= LANE
    vmem = pl.BlockSpec(memory_space=pltpu.VMEM)
    anywhere = pl.BlockSpec(memory_space=pl.ANY)
    wide = pltpu.VMEM((packed, width), F32)
    blocks = pltpu.VMEM((n * 16, width // 2), BF16)
    return pl.pallas_call(
        functools.partial(kernel, n, steps, heads, head_dim),
        out_shape=jax.ShapeDtypeStruct((rows, width), BF16),
        in_specs=[vmem] * 12 + [anywhere] * 2,
        out_specs=vmem,
        scratch_shapes=[wide] * 8
        + [pltpu.VMEM(w_gate_up.shape[1:], BF16), pltpu.VMEM(w_down.shape[1:], BF16)]
        + [blocks] * 4
        + [
            pltpu.VMEM((n * 8, ff), BF16),
            pltpu.SemaphoreType.DMA((2,)),
            pltpu.SemaphoreType.DMA((2,)),
            pltpu.SemaphoreType.DMA((2,)),
            pltpu.SemaphoreType.DMA((2,)),
        ],
        compiler_params=pltpu.CompilerParams(
            collective_id=0, has_side_effects=True, vmem_limit_bytes=56 << 20
        ),
    )(
        hidden_in,
        queries,
        key_rows,
        value_rows,
        output_gate,
        decay_rate,
        write_rate,
        state_cache,
        head_gain.reshape(1, -1),
        post_gain.reshape(1, -1),
        routes,
        route_weight,
        w_gate_up,
        w_down,
    )


def solution(mesh):
    split_rows = P(("groups", "ep"), None)
    in_specs = (
        (split_rows,) * 7
        + (P(("groups", "ep"), None, None, None), P(), P(), split_rows, split_rows)
        + (P("ep", None, None), P("ep", None, None))
    )
    return jax.shard_map(
        per_device, mesh=mesh, in_specs=in_specs, out_specs=split_rows, check_vma=False
    )
```

time: 125 us -> 70.3 us (0.56)
  the two profiles are of different devices: /device:TPU:0 before, /device:TPU:31 now
where the time goes in v1:
time: 70.3 us; the launch traced here: 70 us
  Pallas kernels  62.9 us (89%)
  local copies, waits for them, and re-layouts  7.04 us (10%)
    pallas_call x1, Pallas kernels, per_device(): pl.pallas_call(functools.partial(kernel, n, steps, heads, head_dim), out_...  62.9 us
    unnamed x5, local copies, waits for them, and re-layouts  7.04 us

profile of v1, /device:TPU:31, one launch (start us, length us, event | category | flops | bytes accessed | tf_op | source)
XLA Modules:
  0.0 70.0 jit_solution(17301091989567671468)
XLA Ops:
  0.0 1.4 %copy.15.decay_ref = f32[20,16]{1,0:T(8,128)} copy(f32[20,16]{0,1:T(8,128)} %param.19) | data formatting | bytes 2560 | tf_op args[5]
  1.4 1.4 %copy.16.write_ref = f32[20,16]{1,0:T(8,128)} copy(f32[20,16]{0,1:T(8,128)} %param.20) | data formatting | bytes 2560 | tf_op args[6]
  2.7 1.4 %copy.17.routes_ref = s32[20,10]{1,0:T(8,128)} copy(s32[20,10]{0,1:T(8,128)} %param.24) | data formatting | bytes 1600 | tf_op args[10]
  4.1 1.4 %copy.18.weight_ref = f32[20,10]{1,0:T(8,128)} copy(f32[20,10]{0,1:T(8,128)} %param.25) | data formatting | bytes 1600 | tf_op args[11]
  5.5 62.9 %shard_map.136 = bf16[20,2048]{1,0:T(8,128)(2,1)} custom-call(bf16[20,2048]{1,0:T(8,128)(2,1)} %hidden_ref.1, bf16[20,2048]{1,0:T(8,128)(2,1)} %q_ref.1, bf16[20,2048]{1,0:T(8,128)(2,1)} %k_ref.1, bf16[20,2048]{1,0:T(8,128)(2,1)} %v_ref.1, bf16[20,2048]{1,0:T(8,128)(2,1)} %gate_ref.1, f32[20,16]{1,0:T(8,128)} %copy.15.decay_ref, f32[20,16]{1,0:T(8,128)} %copy.16.write_ref, ...), custom_call_target="tpu_custom_call" | custom-call | tf_op jit(solution)/shard_map/pallas_call | solution.py:289
  68.4 1.5 %copy.20 = bf16[20,2048]{1,0:T(8,128)(2,1)} copy(bf16[20,2048]{1,0:T(8,128)(2,1)} %shard_map.136) | data formatting | bytes 163840

commit v2 on v1

--- a/solution.py
+++ b/solution.py
@@ -73,7 +73,7 @@
 ):
     me = lax.axis_index("ep")
     rows, width = hidden_ref.shape
-    top = routes_ref.shape[1]
+    top = routes_ref.shape[0]
     seqs = rows // steps
     packed = steps * LANE
     half = width // 2
@@ -102,8 +102,9 @@
     v_s[...] = dot(place_b, v_ref[...])
     gate_s[...] = dot(place_b, gate_ref[...])
     spread = (iota((heads, width), 1) // head_dim == iota((heads, width), 0)).astype(F32)
-    a_s[...] = exact_dot(exact_dot(place_f, decay_ref[...]), spread)
-    b_s[...] = exact_dot(exact_dot(place_f, write_ref[...]), spread)
+    last = (((1,), (1,)), ((), ()))
+    a_s[...] = exact_dot(exact_dot(place_f, decay_ref[...], last), spread)
+    b_s[...] = exact_dot(exact_dot(place_f, write_ref[...], last), spread)
     gain = head_gain_ref[...]
     sequence = iota((2 * packed, head_dim), 0) % LANE
 
@@ -142,31 +143,31 @@
             mixed_s[here, cols] = hid_s[here, cols] + attn * norm * gain * (g / (1.0 + jnp.exp(-g)))
 
     def head_group(i, carry):
-        for j in range(2):
-            one_head(2 * i + j)
+        for j in range(4):
+            one_head(4 * i + j)
         return carry
 
-    lax.fori_loop(0, heads // 2, head_group, 0)
+    lax.fori_loop(0, heads // 4, head_group, 0)
     mixed = mixed_s[...]
     factor = lax.rsqrt(jnp.sum(mixed * mixed, -1, keepdims=True) * (1.0 / width) + 1e-06)
     normed = (mixed * factor * post_gain_ref[...]).astype(BF16)
 
-    expert = iota((rows, n), 1)
-    named = jnp.zeros((rows, n), F32)
-    weights = jnp.zeros((rows, n), F32)
+    expert = iota((n, rows), 0)
+    named = jnp.zeros((n, rows), F32)
+    weights = jnp.zeros((n, rows), F32)
     for j in range(top):
-        hit = routes_ref[:, j : j + 1] == expert
+        hit = routes_ref[j : j + 1, :] == expert
         named = jnp.where(hit, 1.0, named)
-        weights = jnp.where(hit, weight_ref[:, j : j + 1], weights)
-    earlier = (iota((rows, rows), 0) >= iota((rows, rows), 1)).astype(BF16)
-    order = named * dot(earlier, named.astype(BF16))
-    order = dot(place_b, order.astype(BF16)).astype(BF16)
-    weights = exact_dot(place_f, weights)
+        weights = jnp.where(hit, weight_ref[j : j + 1, :], weights)
+    earlier = (iota((rows, rows), 0) <= iota((rows, rows), 1)).astype(BF16)
+    order = named * dot(named.astype(BF16), earlier)
+    order = lax.dot_general(order.astype(BF16), place_b, last, preferred_element_type=F32).astype(BF16)
+    weights = exact_dot(weights, place_f, last)
 
     slots = n * 16
     slot_row = iota((slots, n), 0)
     owner = (slot_row // 16 == iota((slots, n), 1)).astype(BF16)
-    found = lax.dot_general(owner, order, (((1,), (1,)), ((), ())), preferred_element_type=F32)
+    found = dot(owner, order)
     slot_at = iota((slots, packed), 0)
     chosen = found == (slot_at % 8 + 1).astype(F32)
     on_left = slot_at % 16 < 8
@@ -181,48 +182,60 @@
     def block(i):
         return pl.ds(pl.multiple_of(i * 16, 16), 16)
 
-    def exchange(source, target, number):
-        def send(i, carry):
-            other = lax.rem(me + i, n)
+    def exchange(source, target, number, cols):
+        group = n // 2
+        mine, low = me // group, lax.rem(me, group)
+
+        def send(other):
             pltpu.make_async_remote_copy(
-                src_ref=source.at[block(other)],
-                dst_ref=target.at[block(me)],
+                src_ref=source.at[block(other), cols],
+                dst_ref=target.at[block(me), cols],
                 send_sem=send_sem.at[number],
                 recv_sem=recv_sem.at[number],
                 device_id={"ep": other},
                 device_id_type=MESH,
             ).start()
+
+        def send_two(i, carry):
+            at = lax.rem(low + i, group)
+            send((1 - mine) * group + at)
+            send(mine * group + at)
             return carry
 
-        lax.fori_loop(1, n, send, 0)
-        own = pltpu.make_async_copy(source.at[block(me)], target.at[block(me)], local_sem.at[number])
+        send((1 - mine) * group + low)
+        lax.fori_loop(1, group, send_two, 0)
+        own = pltpu.make_async_copy(
+            source.at[block(me), cols], target.at[block(me), cols], local_sem.at[number]
+        )
         own.start()
-        own.wait()
         rest = pl.ds(0, (n - 1) * 16)
-        return pltpu.make_async_remote_copy(
-            src_ref=source.at[rest],
-            dst_ref=target.at[rest],
+        others = pltpu.make_async_remote_copy(
+            src_ref=source.at[rest, cols],
+            dst_ref=target.at[rest, cols],
             send_sem=send_sem.at[number],
             recv_sem=recv_sem.at[number],
             device_id={"ep": lax.rem(me + 1, n)},
             device_id_type=MESH,
         )
+        return own, others
 
     pl.semaphore_wait(barrier, n - 1)
-    first = exchange(out_buf, in_buf, 0)
+    first_own, first = exchange(out_buf, in_buf, 0, pl.ds(0, half))
     owner_t = (iota((n, slots), 1) // 16 == iota((n, slots), 0)).astype(BF16)
     lane_slot = iota((packed, slots), 1)
-    taken = dot(order, owner_t) == (lane_slot % 8 + 1).astype(F32)
+    over = (((0,), (0,)), ((), ()))
+    taken = lax.dot_general(order, owner_t, over, preferred_element_type=F32) == (lane_slot % 8 + 1).astype(F32)
     high, low = split(weights)
     lane_left = lane_slot % 16 < 8
     mixing = []
     for part in (high, low):
-        value = dot(part, owner_t)
+        value = lax.dot_general(part, owner_t, over, preferred_element_type=F32)
         mixing.append(jnp.where(taken & lane_left, value, 0.0).astype(BF16))
         mixing.append(jnp.where(taken & ~lane_left, value, 0.0).astype(BF16))
     mix = jnp.concatenate(mixing, 0)
     gate_up_copy.wait()
     down_copy.wait()
+    first_own.wait()
     first.wait_recv()
 
     arrived = in_buf[...].astype(F32).reshape(n, 16, half)
@@ -235,16 +248,20 @@
         up = dot(left_in, gate_up_s[:half, up_at]) + dot(right_in, gate_up_s[half:, up_at])
         hidden_s[:, at] = (gate / (1.0 + jnp.exp(-gate)) * up).astype(BF16)
     units = hidden_s[...]
+    returns = []
     for c in range(half // step):
         at = slice(c * step, (c + 1) * step)
         right_at = slice(half + c * step, half + (c + 1) * step)
         left = dot(units, down_s[:, at]).reshape(n, 8, step)
         right = dot(units, down_s[:, right_at]).reshape(n, 8, step)
         back_buf[:, at] = jnp.concatenate([left, right], 1).reshape(slots, step).astype(BF16)
-    second = exchange(back_buf, ret_buf, 1)
+        if c % 2:
+            returns.append(exchange(back_buf, ret_buf, 1 + c // 2, pl.ds((c - 1) * step, 2 * step)))
     first.wait_send()
-    second.wait_recv()
     for c in range(half // step):
+        if c % 2 == 0:
+            returns[c // 2][0].wait()
+            returns[c // 2][1].wait_recv()
         at = slice(c * step, (c + 1) * step)
         right_at = slice(half + c * step, half + (c + 1) * step)
         sums = dot(mix, ret_buf[:, at])
@@ -253,9 +270,10 @@
         for cols, value in ((at, left), (right_at, right)):
             total = (mixed_s[:, cols] + value).astype(BF16)
             out_ref[:, cols] = lax.dot_general(
-                place_b, total, (((0,), (0,)), ((), ())), preferred_element_type=F32
+                place_b, total, over, preferred_element_type=F32
             ).astype(BF16)
-    second.wait_send()
+    for _, others in returns:
+        others.wait_send()
 
 
 def per_device(
@@ -297,9 +315,9 @@
         + [
             pltpu.VMEM((n * 8, ff), BF16),
             pltpu.SemaphoreType.DMA((2,)),
-            pltpu.SemaphoreType.DMA((2,)),
-            pltpu.SemaphoreType.DMA((2,)),
-            pltpu.SemaphoreType.DMA((2,)),
+            pltpu.SemaphoreType.DMA((4,)),
+            pltpu.SemaphoreType.DMA((4,)),
+            pltpu.SemaphoreType.DMA((4,)),
         ],
         compiler_params=pltpu.CompilerParams(
             collective_id=0, has_side_effects=True, vmem_limit_bytes=56 << 20
@@ -310,13 +328,13 @@
         key_rows,
         value_rows,
         output_gate,
-        decay_rate,
-        write_rate,
+        decay_rate.T,
+        write_rate.T,
         state_cache,
         head_gain.reshape(1, -1),
         post_gain.reshape(1, -1),
-        routes,
-        route_weight,
+        routes.T,
+        route_weight.T,
         w_gate_up,
         w_down,
     )

time: 70.3 us -> 61 us (0.87)
  the two profiles are of different devices: /device:TPU:31 before, /device:TPU:0 now
where the time goes in v2:
time: 61 us; the launch traced here: 60.8 us
  Pallas kernels  59.3 us (97%)
  local copies, waits for them, and re-layouts  1.54 us (3%)
    pallas_call x1, Pallas kernels, per_device(): pl.pallas_call(functools.partial(kernel, n, steps, heads, head_dim), out_...  59.3 us
    unnamed x1, local copies, waits for them, and re-layouts  1.54 us

profile of v2, /device:TPU:0, one launch (start us, length us, event | category | flops | bytes accessed | tf_op | source)
XLA Modules:
  0.0 60.8 jit_solution(12918580054946942784)
XLA Ops:
  0.0 59.3 %shard_map.136 = bf16[20,2048]{1,0:T(8,128)(2,1)} custom-call(bf16[20,2048]{1,0:T(8,128)(2,1)} %hidden_ref.1, bf16[20,2048]{1,0:T(8,128)(2,1)} %q_ref.1, bf16[20,2048]{1,0:T(8,128)(2,1)} %k_ref.1, bf16[20,2048]{1,0:T(8,128)(2,1)} %v_ref.1, bf16[20,2048]{1,0:T(8,128)(2,1)} %gate_ref.1, f32[16,20]{1,0:T(8,128)} %bitcast.6, f32[16,20]{1,0:T(8,128)} %bitcast.7, ...), custom_call_target="tpu_custom_call" | custom-call | tf_op jit(solution)/shard_map/pallas_call | solution.py:307
  59.3 1.5 %copy.16 = bf16[20,2048]{1,0:T(8,128)(2,1)} copy(bf16[20,2048]{1,0:T(8,128)(2,1)} %shard_map.136) | data formatting | bytes 163840

commit v3 on v2

--- a/solution.py
+++ b/solution.py
@@ -43,7 +43,7 @@
     gate_ref,
     decay_ref,
     write_ref,
-    state_ref,
+    state_hbm,
     head_gain_ref,
     post_gain_ref,
     routes_ref,
@@ -61,6 +61,8 @@
     mixed_s,
     gate_up_s,
     down_s,
+    state_s,
+    product_s,
     out_buf,
     in_buf,
     back_buf,
@@ -78,6 +80,8 @@
     packed = steps * LANE
     half = width // 2
     ff = down_s.shape[0]
+    state_copy = pltpu.make_async_copy(state_hbm, state_s, weight_sem.at[2])
+    state_copy.start()
     barrier = pltpu.get_barrier_semaphore()
 
     def greet(i, carry):
@@ -117,7 +121,7 @@
         both = jnp.concatenate([k_all, q_all], 0).astype(BF16)
         reads = jnp.zeros((2 * packed, head_dim), F32)
         for s in range(seqs):
-            reads = jnp.where(sequence == s, dot(both, state_ref[s, h]), reads)
+            reads = jnp.where(sequence == s, dot(both, state_s[s, h]), reads)
         carried = None
         writes, keys = [], []
         for t in range(steps):
@@ -147,6 +151,7 @@
             one_head(4 * i + j)
         return carry
 
+    state_copy.wait()
     lax.fori_loop(0, heads // 4, head_group, 0)
     mixed = mixed_s[...]
     factor = lax.rsqrt(jnp.sum(mixed * mixed, -1, keepdims=True) * (1.0 / width) + 1e-06)
@@ -173,12 +178,6 @@
     on_left = slot_at % 16 < 8
     pick_left = jnp.where(chosen & on_left, 1.0, 0.0).astype(BF16)
     pick_right = jnp.where(chosen & ~on_left, 1.0, 0.0).astype(BF16)
-    step = 256
-    for c in range(half // step):
-        left = normed[:, c * step : (c + 1) * step]
-        right = normed[:, half + c * step : half + (c + 1) * step]
-        out_buf[:, c * step : (c + 1) * step] = (dot(pick_left, left) + dot(pick_right, right)).astype(BF16)
-
     def block(i):
         return pl.ds(pl.multiple_of(i * 16, 16), 16)
 
@@ -219,8 +218,15 @@
         )
         return own, others
 
+    step = half // 4
+    parts = ((0, step), (step, 2 * step), (3 * step, step))
     pl.semaphore_wait(barrier, n - 1)
-    first_own, first = exchange(out_buf, in_buf, 0, pl.ds(0, half))
+    sent = []
+    for number, (start, size) in enumerate(parts):
+        left = normed[:, start : start + size]
+        right = normed[:, half + start : half + start + size]
+        out_buf[:, start : start + size] = (dot(pick_left, left) + dot(pick_right, right)).astype(BF16)
+        sent.append(exchange(out_buf, in_buf, number, pl.ds(start, size)))
     owner_t = (iota((n, slots), 1) // 16 == iota((n, slots), 0)).astype(BF16)
     lane_slot = iota((packed, slots), 1)
     over = (((0,), (0,)), ((), ()))
@@ -235,35 +241,41 @@
     mix = jnp.concatenate(mixing, 0)
     gate_up_copy.wait()
     down_copy.wait()
-    first_own.wait()
-    first.wait_recv()
-
-    arrived = in_buf[...].astype(F32).reshape(n, 16, half)
-    left_in = arrived[:, :8].reshape(n * 8, half).astype(BF16)
-    right_in = arrived[:, 8:].reshape(n * 8, half).astype(BF16)
-    for c in range(ff // step):
-        at = slice(c * step, (c + 1) * step)
-        up_at = slice(ff + c * step, ff + (c + 1) * step)
-        gate = dot(left_in, gate_up_s[:half, at]) + dot(right_in, gate_up_s[half:, at])
-        up = dot(left_in, gate_up_s[:half, up_at]) + dot(right_in, gate_up_s[half:, up_at])
-        hidden_s[:, at] = (gate / (1.0 + jnp.exp(-gate)) * up).astype(BF16)
+    for number, (start, size) in enumerate(parts):
+        sent[number][0].wait()
+        sent[number][1].wait_recv()
+        arrived = in_buf[:, start : start + size].astype(F32).reshape(n, 16, size)
+        left_in = arrived[:, :8].reshape(n * 8, size).astype(BF16)
+        right_in = arrived[:, 8:].reshape(n * 8, size).astype(BF16)
+        left_at, right_at = pl.ds(start, size), pl.ds(half + start, size)
+
+        def product(at):
+            value = dot(left_in, gate_up_s[left_at, at]) + dot(right_in, gate_up_s[right_at, at])
+            return value if number == 0 else product_s[:, at] + value
+
+        for c in range(ff // step):
+            at, up_at = pl.ds(c * step, step), pl.ds(ff + c * step, step)
+            gate, up = product(at), product(up_at)
+            if number + 1 < len(parts):
+                product_s[:, at], product_s[:, up_at] = gate, up
+            else:
+                hidden_s[:, at] = (gate / (1.0 + jnp.exp(-gate)) * up).astype(BF16)
     units = hidden_s[...]
     returns = []
-    for c in range(half // step):
-        at = slice(c * step, (c + 1) * step)
-        right_at = slice(half + c * step, half + (c + 1) * step)
-        left = dot(units, down_s[:, at]).reshape(n, 8, step)
-        right = dot(units, down_s[:, right_at]).reshape(n, 8, step)
-        back_buf[:, at] = jnp.concatenate([left, right], 1).reshape(slots, step).astype(BF16)
-        if c % 2:
-            returns.append(exchange(back_buf, ret_buf, 1 + c // 2, pl.ds((c - 1) * step, 2 * step)))
-    first.wait_send()
-    for c in range(half // step):
-        if c % 2 == 0:
-            returns[c // 2][0].wait()
-            returns[c // 2][1].wait_recv()
-        at = slice(c * step, (c + 1) * step)
-        right_at = slice(half + c * step, half + (c + 1) * step)
+    for number, (start, size) in enumerate(parts):
+        at = slice(start, start + size)
+        right_at = slice(half + start, half + start + size)
+        left = dot(units, down_s[:, at]).reshape(n, 8, size)
+        right = dot(units, down_s[:, right_at]).reshape(n, 8, size)
+        back_buf[:, at] = jnp.concatenate([left, right], 1).reshape(slots, size).astype(BF16)
+        returns.append(exchange(back_buf, ret_buf, len(parts) + number, pl.ds(start, size)))
+    for _, others in sent:
+        others.wait_send()
+    for number, (start, size) in enumerate(parts):
+        returns[number][0].wait()
+        returns[number][1].wait_recv()
+        at = slice(start, start + size)
+        right_at = slice(half + start, half + start + size)
         sums = dot(mix, ret_buf[:, at])
         left = sums[:packed] + sums[2 * packed : 3 * packed]
         right = sums[packed : 2 * packed] + sums[3 * packed :]
@@ -307,17 +319,18 @@
     return pl.pallas_call(
         functools.partial(kernel, n, steps, heads, head_dim),
         out_shape=jax.ShapeDtypeStruct((rows, width), BF16),
-        in_specs=[vmem] * 12 + [anywhere] * 2,
+        in_specs=[vmem] * 7 + [anywhere] + [vmem] * 4 + [anywhere] * 2,
         out_specs=vmem,
         scratch_shapes=[wide] * 8
         + [pltpu.VMEM(w_gate_up.shape[1:], BF16), pltpu.VMEM(w_down.shape[1:], BF16)]
+        + [pltpu.VMEM(state_cache.shape, BF16), pltpu.VMEM((n * 8, 2 * ff), F32)]
         + [blocks] * 4
         + [
             pltpu.VMEM((n * 8, ff), BF16),
-            pltpu.SemaphoreType.DMA((2,)),
-            pltpu.SemaphoreType.DMA((4,)),
-            pltpu.SemaphoreType.DMA((4,)),
-            pltpu.SemaphoreType.DMA((4,)),
+            pltpu.SemaphoreType.DMA((3,)),
+            pltpu.SemaphoreType.DMA((6,)),
+            pltpu.SemaphoreType.DMA((6,)),
+            pltpu.SemaphoreType.DMA((6,)),
         ],
         compiler_params=pltpu.CompilerParams(
             collective_id=0, has_side_effects=True, vmem_limit_bytes=56 << 20

time: 61 us -> 61.8 us (1.013)
  Pallas kernels: 59.3 us -> 60.1 us
    pallas_call x1, Pallas kernels: 59.3 us -> 60.1 us  [per_device(): pl.pallas_call(functools.partial(kernel, n, steps, heads, head_dim), out_...]
where the time goes in v3:
time: 61.8 us; the launch traced here: 61.7 us
  Pallas kernels  60.1 us (97%)
  local copies, waits for them, and re-layouts  1.54 us (2%)
    pallas_call x1, Pallas kernels, per_device(): pl.pallas_call(functools.partial(kernel, n, steps, heads, head_dim), out_...  60.1 us
    unnamed x1, local copies, waits for them, and re-layouts  1.54 us

profile of v3, /device:TPU:0, one launch (start us, length us, event | category | flops | bytes accessed | tf_op | source)
XLA Modules:
  0.0 61.7 jit_solution(9551870693857185857)
XLA Ops:
  0.0 60.1 %shard_map.136 = bf16[20,2048]{1,0:T(8,128)(2,1)} custom-call(bf16[20,2048]{1,0:T(8,128)(2,1)} %hidden_ref.1, bf16[20,2048]{1,0:T(8,128)(2,1)} %q_ref.1, bf16[20,2048]{1,0:T(8,128)(2,1)} %k_ref.1, bf16[20,2048]{1,0:T(8,128)(2,1)} %v_ref.1, bf16[20,2048]{1,0:T(8,128)(2,1)} %gate_ref.1, f32[16,20]{1,0:T(8,128)} %bitcast.6, f32[16,20]{1,0:T(8,128)} %bitcast.7, ...), custom_call_target="tpu_custom_call" | custom-call | tf_op jit(solution)/shard_map/pallas_call | solution.py:319
  60.1 1.5 %copy.16 = bf16[20,2048]{1,0:T(8,128)(2,1)} copy(bf16[20,2048]{1,0:T(8,128)(2,1)} %shard_map.136) | data formatting | bytes 163840

commit v4 on v2

--- a/solution.py
+++ b/solution.py
@@ -43,7 +43,7 @@
     gate_ref,
     decay_ref,
     write_ref,
-    state_ref,
+    state_hbm,
     head_gain_ref,
     post_gain_ref,
     routes_ref,
@@ -61,6 +61,7 @@
     mixed_s,
     gate_up_s,
     down_s,
+    state_s,
     out_buf,
     in_buf,
     back_buf,
@@ -78,6 +79,8 @@
     packed = steps * LANE
     half = width // 2
     ff = down_s.shape[0]
+    state_copy = pltpu.make_async_copy(state_hbm, state_s, weight_sem.at[2])
+    state_copy.start()
     barrier = pltpu.get_barrier_semaphore()
 
     def greet(i, carry):
@@ -117,7 +120,7 @@
         both = jnp.concatenate([k_all, q_all], 0).astype(BF16)
         reads = jnp.zeros((2 * packed, head_dim), F32)
         for s in range(seqs):
-            reads = jnp.where(sequence == s, dot(both, state_ref[s, h]), reads)
+            reads = jnp.where(sequence == s, dot(both, state_s[s, h]), reads)
         carried = None
         writes, keys = [], []
         for t in range(steps):
@@ -147,6 +150,7 @@
             one_head(4 * i + j)
         return carry
 
+    state_copy.wait()
     lax.fori_loop(0, heads // 4, head_group, 0)
     mixed = mixed_s[...]
     factor = lax.rsqrt(jnp.sum(mixed * mixed, -1, keepdims=True) * (1.0 / width) + 1e-06)
@@ -248,20 +252,17 @@
         up = dot(left_in, gate_up_s[:half, up_at]) + dot(right_in, gate_up_s[half:, up_at])
         hidden_s[:, at] = (gate / (1.0 + jnp.exp(-gate)) * up).astype(BF16)
     units = hidden_s[...]
-    returns = []
     for c in range(half // step):
         at = slice(c * step, (c + 1) * step)
         right_at = slice(half + c * step, half + (c + 1) * step)
         left = dot(units, down_s[:, at]).reshape(n, 8, step)
         right = dot(units, down_s[:, right_at]).reshape(n, 8, step)
         back_buf[:, at] = jnp.concatenate([left, right], 1).reshape(slots, step).astype(BF16)
-        if c % 2:
-            returns.append(exchange(back_buf, ret_buf, 1 + c // 2, pl.ds((c - 1) * step, 2 * step)))
+    second_own, second = exchange(back_buf, ret_buf, 1, pl.ds(0, half))
     first.wait_send()
+    second_own.wait()
+    second.wait_recv()
     for c in range(half // step):
-        if c % 2 == 0:
-            returns[c // 2][0].wait()
-            returns[c // 2][1].wait_recv()
         at = slice(c * step, (c + 1) * step)
         right_at = slice(half + c * step, half + (c + 1) * step)
         sums = dot(mix, ret_buf[:, at])
@@ -272,8 +273,7 @@
             out_ref[:, cols] = lax.dot_general(
                 place_b, total, over, preferred_element_type=F32
             ).astype(BF16)
-    for _, others in returns:
-        others.wait_send()
+    second.wait_send()
 
 
 def per_device(
@@ -307,17 +307,18 @@
     return pl.pallas_call(
         functools.partial(kernel, n, steps, heads, head_dim),
         out_shape=jax.ShapeDtypeStruct((rows, width), BF16),
-        in_specs=[vmem] * 12 + [anywhere] * 2,
+        in_specs=[vmem] * 7 + [anywhere] + [vmem] * 4 + [anywhere] * 2,
         out_specs=vmem,
         scratch_shapes=[wide] * 8
         + [pltpu.VMEM(w_gate_up.shape[1:], BF16), pltpu.VMEM(w_down.shape[1:], BF16)]
+        + [pltpu.VMEM(state_cache.shape, BF16)]
         + [blocks] * 4
         + [
             pltpu.VMEM((n * 8, ff), BF16),
+            pltpu.SemaphoreType.DMA((3,)),
             pltpu.SemaphoreType.DMA((2,)),
-            pltpu.SemaphoreType.DMA((4,)),
-            pltpu.SemaphoreType.DMA((4,)),
-            pltpu.SemaphoreType.DMA((4,)),
+            pltpu.SemaphoreType.DMA((2,)),
+            pltpu.SemaphoreType.DMA((2,)),
         ],
         compiler_params=pltpu.CompilerParams(
             collective_id=0, has_side_effects=True, vmem_limit_bytes=56 << 20

time: 61 us -> 60.6 us (level)
  Pallas kernels: 59.3 us -> 58.4 us
    pallas_call x1, Pallas kernels: 59.3 us -> 58.4 us  [per_device(): pl.pallas_call(functools.partial(kernel, n, steps, heads, head_dim), out_...]
where the time goes in v4:
time: 60.6 us; the launch traced here: 59.9 us
  Pallas kernels  58.4 us (96%)
  local copies, waits for them, and re-layouts  1.54 us (3%)
    pallas_call x1, Pallas kernels, per_device(): pl.pallas_call(functools.partial(kernel, n, steps, heads, head_dim), out_...  58.4 us
    unnamed x1, local copies, waits for them, and re-layouts  1.54 us

profile of v4, /device:TPU:0, one launch (start us, length us, event | category | flops | bytes accessed | tf_op | source)
XLA Modules:
  0.0 59.9 jit_solution(299523221693266111)
XLA Ops:
  0.0 58.4 %shard_map.136 = bf16[20,2048]{1,0:T(8,128)(2,1)} custom-call(bf16[20,2048]{1,0:T(8,128)(2,1)} %hidden_ref.1, bf16[20,2048]{1,0:T(8,128)(2,1)} %q_ref.1, bf16[20,2048]{1,0:T(8,128)(2,1)} %k_ref.1, bf16[20,2048]{1,0:T(8,128)(2,1)} %v_ref.1, bf16[20,2048]{1,0:T(8,128)(2,1)} %gate_ref.1, f32[16,20]{1,0:T(8,128)} %bitcast.6, f32[16,20]{1,0:T(8,128)} %bitcast.7, ...), custom_call_target="tpu_custom_call" | custom-call | tf_op jit(solution)/shard_map/pallas_call | solution.py:307
  58.4 1.5 %copy.16 = bf16[20,2048]{1,0:T(8,128)(2,1)} copy(bf16[20,2048]{1,0:T(8,128)(2,1)} %shard_map.136) | data formatting | bytes 163840

commit v5 on v4

--- a/solution.py
+++ b/solution.py
@@ -146,12 +146,12 @@
             mixed_s[here, cols] = hid_s[here, cols] + attn * norm * gain * (g / (1.0 + jnp.exp(-g)))
 
     def head_group(i, carry):
-        for j in range(4):
-            one_head(4 * i + j)
+        for j in range(8):
+            one_head(8 * i + j)
         return carry
 
     state_copy.wait()
-    lax.fori_loop(0, heads // 4, head_group, 0)
+    lax.fori_loop(0, heads // 8, head_group, 0)
     mixed = mixed_s[...]
     factor = lax.rsqrt(jnp.sum(mixed * mixed, -1, keepdims=True) * (1.0 / width) + 1e-06)
     normed = (mixed * factor * post_gain_ref[...]).astype(BF16)

time: 60.6 us -> 60.5 us (level)
  no operation moved by 1% of the time
where the time goes in v5:
time: 60.5 us; the launch traced here: 59.9 us
  Pallas kernels  58.4 us (97%)
  local copies, waits for them, and re-layouts  1.54 us (3%)
    pallas_call x1, Pallas kernels, per_device(): pl.pallas_call(functools.partial(kernel, n, steps, heads, head_dim), out_...  58.4 us
    unnamed x1, local copies, waits for them, and re-layouts  1.54 us

profile of v5, /device:TPU:0, one launch (start us, length us, event | category | flops | bytes accessed | tf_op | source)
XLA Modules:
  0.0 59.9 jit_solution(17007677397860128627)
XLA Ops:
  0.0 58.4 %shard_map.136 = bf16[20,2048]{1,0:T(8,128)(2,1)} custom-call(bf16[20,2048]{1,0:T(8,128)(2,1)} %hidden_ref.1, bf16[20,2048]{1,0:T(8,128)(2,1)} %q_ref.1, bf16[20,2048]{1,0:T(8,128)(2,1)} %k_ref.1, bf16[20,2048]{1,0:T(8,128)(2,1)} %v_ref.1, bf16[20,2048]{1,0:T(8,128)(2,1)} %gate_ref.1, f32[16,20]{1,0:T(8,128)} %bitcast.6, f32[16,20]{1,0:T(8,128)} %bitcast.7, ...), custom_call_target="tpu_custom_call" | custom-call | tf_op jit(solution)/shard_map/pallas_call | solution.py:307
  58.4 1.5 %copy.16 = bf16[20,2048]{1,0:T(8,128)(2,1)} copy(bf16[20,2048]{1,0:T(8,128)(2,1)} %shard_map.136) | data formatting | bytes 163840
